TPU v7x, 32 devices: a whole 2x2x4 slice. The times are simulated.
32 devices in a mesh: section: 4 (over y, x), dom: 8 (over z, core).
Axes of the slice: x: 2, y: 2, z: 4, core: 2. Of those that a mesh axis runs over, the one named last changes fastest.
Arguments:
- measures: bfloat16 [131072, 128], P(('section', 'dom')), may hold values from -6 to 6
- pred_columns: int32 [2, 131072], P(None, ('section', 'dom')), may hold values from 0 to 99
- bounds: int32 [2, 2], replicated, may hold values from 0 to 100
- lengths: int32 [1024], P(('section', 'dom')), may hold values from 120 to 128
- destination: int32 [131072, 1], P(('section', 'dom')), may hold values from 0 to 31; in each aligned block of 4096 rows (0 to 4095, 4096 to 8191, ...) at most 256 rows name the same one
- key_offset: int32 [131072], P(('section', 'dom')), may hold values from 0 to 2047
- group_ids: int32 [131072], P(('section', 'dom')), may hold values from 0 to 1023
- build_table: bfloat16 [65536, 128], P(('section', 'dom')), may hold values from -6 to 6
Outputs:
- group_sums: float32 [1024, 128], P(('section', 'dom'))
- top_scores: float32 [16], replicated
Inputs may be any that keep to these rules, and one draw needn't show every extreme that they name: Among the rows of one device, no destination is named more than 256 times, a bound that some block reaches.
All inputs are finite; a program needn't handle non-finite values.
Results may differ from a plain program's by a relative error of at most 0.0048.
Values may be sent and summed in bfloat16 or wider, within the bound.
A program may use at most 64 MiB of HBM per device.

v0:
```python
import jax
import jax.numpy as jnp
from jax import lax
from jax.sharding import PartitionSpec as P

BLOCK = 128
TOPK = 16
GRP_DEV = 32


def slot_positions(targets, count_targets):
    matches = (targets[:, None] == jnp.arange(count_targets, dtype=jnp.int32)[None, :]).astype(
        jnp.int32
    )
    before = jnp.cumsum(matches, axis=0) - 1
    return jnp.sum(before * matches, axis=1)


def fill_slots(places, total_slots, payload, first_ints, second_ints):
    payload_buffer = (
        jnp.zeros((total_slots, payload.shape[1]), payload.dtype).at[places].set(payload)
    )
    first_buffer = jnp.zeros((total_slots,), jnp.int32).at[places].set(first_ints)
    second_buffer = jnp.zeros((total_slots,), jnp.int32).at[places].set(second_ints)
    return (payload_buffer, first_buffer, second_buffer)


def join_owned(received, local_keys, build_table, block_rows):
    feat_width = received.shape[1]
    blocks_payload = received.reshape(-1, block_rows, feat_width)
    blocks_keys = local_keys.reshape(-1, block_rows)

    def one_block(members):
        payload_part, keys_part = members
        picker = (
            keys_part[:, None] == jnp.arange(build_table.shape[0], dtype=jnp.int32)[None, :]
        ).astype(jnp.bfloat16)
        fetched = jnp.dot(picker, build_table, preferred_element_type=jnp.float32)
        return (payload_part.astype(jnp.float32) * fetched).astype(jnp.bfloat16)

    joined = lax.map(one_block, (blocks_payload, blocks_keys))
    return joined.reshape(received.shape)


def group_terms(joined, received_groups, count, block_rows):
    feat_width = joined.shape[1]
    blocks_joined = joined.reshape(-1, block_rows, feat_width)
    blocks_groups = received_groups.reshape(-1, block_rows)
    labels = jnp.arange(count, dtype=jnp.int32)

    def add_block(running, members):
        joined_part, group_part = members
        picker = (labels[:, None] == group_part[None, :]).astype(jnp.bfloat16)
        return (running + jnp.dot(picker, joined_part, preferred_element_type=jnp.float32), None)

    running, unused = lax.scan(
        add_block, jnp.zeros((count, feat_width), jnp.float32), (blocks_joined, blocks_groups)
    )
    return running


def on_device(
    measures, pred_columns, bounds, lengths, destination, key_offset, group_ids, build_table
):
    row_count = measures.shape[0]
    feat_width = measures.shape[1]
    devices = lax.axis_size(("section", "dom"))
    within = (lengths[:, None] > jnp.arange(BLOCK, dtype=jnp.int32)[None, :]).reshape(row_count)
    passes = jnp.all((pred_columns >= bounds[:, 0:1]) & (pred_columns < bounds[:, 1:2]), axis=0)
    usable = within & passes
    payload = jnp.where(usable[:, None], measures, jnp.zeros_like(measures))
    targets = destination[:, 0]
    capacity = 2 * row_count // devices
    total_slots = devices * capacity
    places = targets * capacity + slot_positions(targets, devices)
    buffers = fill_slots(places, total_slots, payload, key_offset, group_ids)
    shaped = (
        buffers[0].reshape(devices, capacity, feat_width),
        buffers[1].reshape(devices, capacity),
        buffers[2].reshape(devices, capacity),
    )
    arrived = (
        lax.all_to_all(shaped[0], ("section", "dom"), split_axis=0, concat_axis=0, tiled=True),
        lax.all_to_all(shaped[1], ("section", "dom"), split_axis=0, concat_axis=0, tiled=True),
        lax.all_to_all(shaped[2], ("section", "dom"), split_axis=0, concat_axis=0, tiled=True),
    )
    received = arrived[0].reshape(total_slots, feat_width)
    received_keys = arrived[1].reshape(total_slots)
    received_groups = arrived[2].reshape(total_slots)
    block_rows = 1024
    joined = join_owned(received, received_keys, build_table, block_rows)
    group_sums = lax.psum_scatter(
        group_terms(
            joined, received_groups, GRP_DEV * lax.axis_size(("section", "dom")), block_rows
        ),
        ("section", "dom"),
        scatter_dimension=0,
        tiled=True,
    )
    scores = jnp.mean(group_sums, axis=1)
    everything = lax.all_gather(scores, ("section", "dom"), axis=0, tiled=True)
    leaders = lax.top_k(everything, TOPK)[0]
    return (group_sums, leaders)


def solution(mesh):
    return jax.shard_map(
        on_device,
        mesh=mesh,
        in_specs=(
            P(("section", "dom"), None),
            P(None, ("section", "dom")),
            P(),
            P(("section", "dom")),
            P(("section", "dom"), None),
            P(("section", "dom")),
            P(("section", "dom")),
            P(("section", "dom"), None),
        ),
        out_specs=(P(("section", "dom"), None), P()),
        check_vma=False,
    )
```

profile of v0, /device:TPU:0, one launch (start us, length us, event | category | flops | bytes accessed | tf_op | source)
XLA Modules:
  0.0 351.0 jit_solution(2472670084108107789)
XLA Ops:
  7.2 0.9 fusion.21
  8.1 9.2 %reduce-window.6 = s32[32,32,128]{2,1,0:T(8,128)S(1)} reduce-window(s32[32,32,128]{2,1,0:T(8,128)S(1)} %fusion.21, s32[]{:T(128)} %constant.44.clone.1), window={size=1x1x128 pad=0_0x0_0x127_0}, to_apply=%region_0.0 | reduce-window | flops 16646144 | bytes 1048580 | tf_op jit(solution)/shard_map/reduce-window
  17.3 0.8 slice_reduce_fusion
  18.9 16.3 %scatter_custom_fusion.2 = s32[8192]{0:T(1024)} fusion(s32[4096]{0:T(1024)S(1)} %bitcast.59, s32[4096]{0:T(1024)} %param.17, s32[]{:T(128)} %constant.44.clone.1), kind=kCustom, calls=%fused_computation.36 | custom fusion | bytes 33280 | tf_op jit(solution)/shard_map/scatter | solution.py:23
  35.2 7.3 %all-to-all-start.2 = ((s32[32,1,256]{2,1,0:T(1,128)}), s32[32,1,256]{2,1,0:T(1,128)S(1)}, u32[]{:S(2)}, u32[]{:S(2)}) async-start(s32[32,1,256]{2,1,0:T(1,128)} %bitcast.12), calls=%async_computation.2 | async-start | bytes 65536 | tf_op jit(solution)/shard_map/all_to_all | solution.py:84
  42.6 16.3 %scatter_custom_fusion = s32[8192]{0:T(1024)} fusion(s32[4096]{0:T(1024)S(1)} %bitcast.60, s32[4096]{0:T(1024)} %param.18, s32[]{:T(128)} %constant.44.clone.1), kind=kCustom, calls=%fused_computation.38 | custom fusion | bytes 33280 | tf_op jit(solution)/shard_map/scatter | solution.py:24
  59.0 5.8 %all-to-all-start = ((s32[32,1,256]{2,1,0:T(1,128)}), s32[32,1,256]{2,1,0:T(1,128)S(1)}, u32[]{:S(2)}, u32[]{:S(2)}) async-start(s32[32,1,256]{2,1,0:T(1,128)} %bitcast.8), calls=%async_computation | async-start | bytes 65536 | tf_op jit(solution)/shard_map/all_to_all | solution.py:85
  65.0 14.6 %scatter_custom_fusion.1 = bf16[8192,128]{1,0:T(8,128)(2,1)} fusion(s32[4096]{0:T(1024)S(1)} %bitcast.61, bf16[4096,128]{1,0:T(8,128)(2,1)S(1)} %copy-done, bf16[]{:T(256)} %constant.46.clone.1, pred[4096]{0:T(1024)(128)(4,1)S(1)} %fusion.27), kind=kCustom, calls=%fused_computation.20 | custom fusion | flops 524288 | bytes 3150848 | tf_op jit(solution)/shard_map/scatter | solution.py:21
  79.6 5.8 %all-to-all-start.1 = ((bf16[32,256,128]{2,1,0:T(8,128)(2,1)}), bf16[32,256,128]{2,1,0:T(8,128)(2,1)S(1)}, u32[]{:S(2)}, u32[]{:S(2)}) async-start(bf16[32,256,128]{2,1,0:T(8,128)(2,1)} %bitcast.10), calls=%async_computation.1 | async-start | bytes 4194304 | tf_op jit(solution)/shard_map/all_to_all | solution.py:83
  85.7 49.8 %all-to-all-done.1 = bf16[32,256,128]{2,1,0:T(8,128)(2,1)S(1)} async-done(((bf16[32,256,128]{2,1,0:T(8,128)(2,1)}), bf16[32,256,128]{2,1,0:T(8,128)(2,1)S(1)}, u32[]{:S(2)}, u32[]{:S(2)}) %all-to-all-start.1) | async-done | bytes 2097184 | tf_op jit(solution)/shard_map/all_to_all | solution.py:83
  135.6 17.7 %while.21 = (s32[]{:T(128)}, bf16[8,1024,128]{2,1,0:T(8,128)(2,1)}, bf16[8,1024,128]{2,1,0:T(8,128)(2,1)S(1)}, s32[8,1024]{1,0:T(8,128)S(1)}, bf16[2048,128]{1,0:T(8,128)(2,1)S(1)}, /*index=5*/s32[]{:T(128)}) while((s32[]{:T(128)}, bf16[8,1024,128]{2,1,0:T(8,128)(2,1)}, bf16[8,1024,128]{2,1,0:T(8,128)(2,1)S(1)}, s32[8,1024]{1,0:T(8,128)S(1)}, ...), condition=%wide.region_7.8_spmd, body=%wide.region_6.7_spmd.sunk | while | flops 539361280 | bytes 1061449 | solution.py:41
  135.6 2.2 fusion.34
  137.8 2.2 fusion.34
  140.0 2.2 fusion.34
  142.2 2.2 fusion.34
  144.4 2.2 fusion.34
  146.6 2.2 fusion.34
  148.9 2.2 fusion.34
  151.1 2.2 fusion.34
  153.3 15.4 %while.22 = (s32[]{:T(128)}, f32[1024,128]{1,0:T(8,128)S(1)}, s32[8,1024]{1,0:T(8,128)S(1)}, bf16[8,1024,128]{2,1,0:T(8,128)(2,1)}, s32[]{:T(128)}, /*index=5*/s32[]{:T(128)}) while((s32[]{:T(128)}, f32[1024,128]{1,0:T(8,128)S(1)}, s32[8,1024]{1,0:T(8,128)S(1)}, bf16[8,1024,128]{2,1,0:T(8,128)(2,1)}, s32[]{:T(128)}, ...), condition=%wide.region_10.11_spmd.clone, body=%wide.region_9.10_spmd.clone.sunk | while | flops 269746176 | bytes 1323603 | solution.py:56
  153.3 1.9 fusion.36
  155.2 1.9 fusion.36
  157.2 1.9 fusion.36
  159.1 1.9 fusion.36
  161.0 1.9 fusion.36
  163.0 1.9 fusion.36
  164.9 1.9 fusion.36
  166.8 1.9 fusion.36
  169.6 131.8 %reduce-scatter.2.cloned.1.call-done = f32[32,128]{1,0:T(8,128)} async-done(((f32[1024,128]{1,0:T(8,128)}), f32[32,128]{1,0:T(8,128)}) %reduce-scatter.2.cloned.1.call-update) | async-done | bytes 16400 | tf_op jit(solution)/shard_map/reduce_scatter | solution.py:92
  301.4 0.8 reduce_sum.22
  302.3 36.9 %all-reduce = f32[1024]{0:T(1024)S(1)} all-reduce(f32[1024]{0:T(1024)S(1)} %multiply_dynamic-update-slice_fusion), channel_id=1, replica_groups=mesh['section'=4,'dom'=8] {'section','dom'}, use_global_device_ids=true, to_apply=%add | all-reduce | flops 1024 | bytes 8192
  339.2 4.4 %top_k.9 = (f32[1024]{0:T(1024)S(1)}, s32[1024]{0:T(1024)}) sort(f32[1024]{0:T(1024)S(1)} %all-reduce, s32[1024]{0:T(1024)S(1)} %iota.23), dimensions={0}, to_apply=%region_13.14 | sort | flops 10240 | bytes 16384 | tf_op jit(solution)/shard_map/top_k | solution.py:102
  (51 shorter events, 2.9 us)
Async XLA Ops:
  7.2 11.3 %copy-start.2 = (s32[4096,1]{0,1:T(1,128)S(1)}, s32[4096,1]{0,1:T(1,128)}, u32[]{:S(2)}) copy-start(s32[4096,1]{0,1:T(1,128)} %param.16) | copy-start | bytes 49156
  7.2 35.3 %copy-start.4 = (s32[2,2]{1,0:T(2,128)S(1)}, s32[2,2]{1,0:T(2,128)}, u32[]{:S(2)}) copy-start(s32[2,2]{1,0:T(2,128)} %param.14) | copy-start | bytes 52
  7.2 51.7 %copy-start.3 = (s32[2,4096]{1,0:T(2,128)S(1)}, s32[2,4096]{1,0:T(2,128)}, u32[]{:S(2)}) copy-start(s32[2,4096]{1,0:T(2,128)} %param.13) | copy-start | bytes 98308
  7.2 57.7 %copy-start.5 = (s32[32]{0:T(128)S(1)}, s32[32]{0:T(128)}, u32[]{:S(2)}) copy-start(s32[32]{0:T(128)} %param.15) | copy-start | bytes 388
  7.2 57.8 %copy-start = (bf16[4096,128]{1,0:T(8,128)(2,1)S(1)}, bf16[4096,128]{1,0:T(8,128)(2,1)}, u32[]{:S(2)}) copy-start(bf16[4096,128]{1,0:T(8,128)(2,1)} %param.12) | copy-start | bytes 3145732
  35.2 23.9 %all-to-all-start.2 = ((s32[32,1,256]{2,1,0:T(1,128)}), s32[32,1,256]{2,1,0:T(1,128)S(1)}, u32[]{:S(2)}, u32[]{:S(2)}) async-start(s32[32,1,256]{2,1,0:T(1,128)} %bitcast.12), calls=%async_computation.2 | async-start | bytes 65536 | tf_op jit(solution)/shard_map/all_to_all | solution.py:84
  59.0 20.6 %all-to-all-start = ((s32[32,1,256]{2,1,0:T(1,128)}), s32[32,1,256]{2,1,0:T(1,128)S(1)}, u32[]{:S(2)}, u32[]{:S(2)}) async-start(s32[32,1,256]{2,1,0:T(1,128)} %bitcast.8), calls=%async_computation | async-start | bytes 65536 | tf_op jit(solution)/shard_map/all_to_all | solution.py:85
  79.6 56.0 %copy-start.6 = (bf16[2048,128]{1,0:T(8,128)(2,1)S(1)}, bf16[2048,128]{1,0:T(8,128)(2,1)}, u32[]{:S(2)}) copy-start(bf16[2048,128]{1,0:T(8,128)(2,1)} %param.19) | copy-start | bytes 1572868
  79.6 55.9 %all-to-all-start.1 = ((bf16[32,256,128]{2,1,0:T(8,128)(2,1)}), bf16[32,256,128]{2,1,0:T(8,128)(2,1)S(1)}, u32[]{:S(2)}, u32[]{:S(2)}) async-start(bf16[32,256,128]{2,1,0:T(8,128)(2,1)} %bitcast.10), calls=%async_computation.1 | async-start | bytes 4194304 | tf_op jit(solution)/shard_map/all_to_all | solution.py:83
  85.5 215.9 %reduce-scatter.2.cloned.1.call-start = ((), (), s32[]{:S(2)}) async-start(), calls=%async_computation.4 | async-start | bytes 540672 | tf_op jit(solution)/shard_map/reduce_scatter | solution.py:92
  168.7 0.8 copy-start.1
Sparse Core Ops, SparseCore 0:
  169.7 131.6 reduce-scatter.1
where the time goes:
time: 352 us; the launch traced here: 351 us
  waiting for transfers between devices  182 us (52%)
  blocking collectives  36.9 us (10%)
  local copies, waits for them, and re-layouts  35 us (10%)
  matrix products  32.8 us (9%)
  other arithmetic  31.2 us (9%)
  starting transfers between devices  19 us (5%)
  between operations  14.2 us (4%)
    reduce_scatter x1, waiting for transfers between devices, on_device(): lax.psum_scatter(group_terms(joined, received_groups, GRP_DEV * lax.axis_...  132 us
    all_to_all x1, waiting for transfers between devices, on_device(): lax.all_to_all(shaped[0], ('section', 'dom'), split_axis=0, concat_axis=0...  49.8 us
    unnamed x1, blocking collectives  36.9 us
    dot_general x8, matrix products, one_block(): fetched = jnp.dot(picker, build_table, preferred_element_type=jnp.float32)  17.7 us
    scatter x1, local copies, waits for them, and re-layouts, fill_slots(): jnp.zeros((total_slots,), jnp.int32).at[places].set(second_ints)  16.3 us
    scatter x1, local copies, waits for them, and re-layouts, fill_slots(): jnp.zeros((total_slots,), jnp.int32).at[places].set(first_ints)  16.3 us
    dot_general x8, matrix products, add_block(): jnp.dot(picker, joined_part, preferred_element_type=jnp.float32)  15.1 us
    scatter x1, other arithmetic, fill_slots(): jnp.zeros((total_slots, payload.shape[1]), payload.dtype).at[places]  14.6 us
  transfers between devices with their start and end apart: 4, of which 2 were waited for; matrix products, arithmetic and copies ran while one was open for 9% of the time, Pallas kernels for 0%

commit v1 on v0

v1 whole, which is shorter than its diff:
```python
import functools

import jax
import jax.numpy as jnp
from jax import lax
from jax.experimental import pallas as pl
from jax.experimental.pallas import tpu as pltpu
from jax.sharding import PartitionSpec as P

BLOCK = 128
TOPK = 16
GRP_DEV = 32
STRIDE = 11
LOW = 256
MESH = pl.DeviceIdType.MESH
F32 = jnp.float32
BF16 = jnp.bfloat16


def iota(shape, dim, dtype=jnp.int32):
    return lax.broadcasted_iota(jnp.int32, shape, dim).astype(dtype)


def one_hot(condition, dtype=BF16):
    return jnp.where(condition, jnp.ones((), F32), jnp.zeros((), F32)).astype(dtype)


def kernel(
    devices,
    inner,
    cap,
    bounds_ref,
    lengths_ref,
    x_ref,
    pred_ref,
    dest_ref,
    key_ref,
    group_ref,
    table_ref,
    sums_ref,
    top_ref,
    onehot,
    dest_wide,
    masked_meta,
    meta_tiles,
    table_wide,
    send_buf,
    recv_buf,
    acc,
    acc_send,
    part_recv,
    score_send,
    score_recv,
    send_sem,
    recv_sem,
    part_send_sem,
    part_recv_sem,
    score_send_sem,
    score_recv_sem,
):
    rows, width = x_ref.shape
    blocks = rows // BLOCK
    parts = cap // BLOCK
    groups = acc.shape[0]
    high = table_ref.shape[0] // LOW
    me = lax.axis_index("section") * inner + lax.axis_index("dom")

    def partner(step):
        return lax.rem(me + STRIDE * step, devices)

    def address(index):
        return (lax.div(index, inner), lax.rem(index, inner))

    barrier = pltpu.get_barrier_semaphore()

    @pl.loop(1, devices)
    def _(step):
        pl.semaphore_signal(
            barrier, inc=1, device_id=address(partner(step)), device_id_type=MESH
        )

    names = iota((devices, BLOCK), 0)
    matches = [
        (dest_ref[b : b + 1, :] == names).astype(F32) for b in range(blocks)
    ]
    stacked = jnp.concatenate(matches, axis=0).astype(BF16)
    upto = one_hot(iota((BLOCK, BLOCK), 0) <= iota((BLOCK, BLOCK), 1))
    adders = jnp.concatenate([upto, jnp.ones((BLOCK, BLOCK), BF16)], axis=1)
    counts = jnp.dot(stacked, adders, preferred_element_type=F32)
    before = jnp.zeros((devices, BLOCK), F32)
    slots = iota((cap, BLOCK), 0, F32)
    lane = iota((1, BLOCK), 1)
    diagonal = iota((BLOCK, BLOCK), 0) == iota((BLOCK, BLOCK), 1)
    ones = jnp.ones((BLOCK, BLOCK), BF16)
    for b in range(blocks):
        part = counts[b * devices : (b + 1) * devices]
        place = (
            jnp.sum(matches[b] * (part[:, :BLOCK] + before), axis=0, keepdims=True) - 1.0
        )
        before = before + part[:, BLOCK:]
        columns = slice(b * BLOCK, (b + 1) * BLOCK)
        usable = lane < lengths_ref[b]
        for c in range(pred_ref.shape[0]):
            values = pred_ref[c : c + 1, columns]
            usable = usable & (values >= bounds_ref[c, 0]) & (values < bounds_ref[c, 1])
        place = jnp.where(usable, place, -1.0)
        onehot[:, columns] = one_hot(slots == place)
        dest_row = dest_ref[b : b + 1, :].astype(F32)
        dest_diag = jnp.where(diagonal, dest_row, 0.0).astype(BF16)
        dest_wide[columns, :] = jnp.dot(
            dest_diag, ones, preferred_element_type=F32
        ).astype(BF16)
        key = key_ref[b : b + 1, :]
        group = group_ref[b : b + 1, :]
        row8 = iota((16, BLOCK), 0) % 8
        meta = jnp.where(row8 == 0, key // LOW, 0)
        meta = jnp.where(row8 == 1, key % LOW, meta)
        meta = jnp.where(row8 == 2, group // 64, meta)
        meta = jnp.where(row8 == 3, group % 64, meta).astype(F32)
        pair = iota((16, BLOCK), 0) // 8
        for d in range(0, devices, 2):
            masked_meta[d * 8 : d * 8 + 16, columns] = jnp.where(
                dest_ref[b : b + 1, :] == pair + d, meta, 0.0
            ).astype(BF16)
    meta_all = lax.dot_general(
        masked_meta[...], onehot[...], (((1,), (1,)), ((), ())), preferred_element_type=F32
    )
    meta_rows = meta_tiles.shape[1]
    for d in range(devices):
        tiles = [
            meta_all[d * 8 : d * 8 + 8, p * BLOCK : (p + 1) * BLOCK] for p in range(parts)
        ]
        if parts * 8 < meta_rows:
            tiles.append(jnp.zeros((meta_rows - parts * 8, BLOCK), F32))
        meta_tiles[d] = jnp.concatenate(tiles, axis=0).astype(BF16)
    for h in range(high):
        table_wide[:, h * width : (h + 1) * width] = table_ref[h * LOW : (h + 1) * LOW, :]

    pl.semaphore_wait(barrier, devices - 1)

    def row_copy(step):
        return pltpu.make_async_remote_copy(
            src_ref=send_buf.at[step],
            dst_ref=recv_buf.at[step],
            send_sem=send_sem.at[step],
            recv_sem=recv_sem.at[step],
            device_id=address(partner(step)),
            device_id_type=MESH,
        )

    @pl.loop(0, devices // 2)
    def _(index):
        first = 2 * index + 1
        second = lax.rem(first + 1, devices)
        wide = dest_wide[...]
        sides = []
        for step in (first, second):
            name = partner(step).astype(F32).astype(BF16)
            sides.append(jnp.where(wide == name, x_ref[...], jnp.zeros((), BF16)))
        placed = jnp.dot(
            onehot[...], jnp.concatenate(sides, axis=1), preferred_element_type=F32
        ).astype(BF16)
        for at, step in enumerate((first, second)):
            send_buf[step, 0:cap, :] = placed[:, at * width : (at + 1) * width]
            send_buf[step, cap:, :] = meta_tiles[partner(step)]
        row_copy(first).start()

        @pl.when(second > 0)
        def _():
            row_copy(second).start()

    def join_block(buf, step, started):
        payload = buf[step, 0:cap, :].astype(F32)
        tile = buf[step, cap:, :]
        across = tile.astype(F32)
        down = lax.dot_general(
            one_hot(diagonal), tile, (((1,), (1,)), ((), ())), preferred_element_type=F32
        )
        key_high = jnp.concatenate([down[:, 8 * p : 8 * p + 1] for p in range(parts)], axis=0)
        key_low = jnp.concatenate(
            [down[:, 8 * p + 1 : 8 * p + 2] for p in range(parts)], axis=0
        )
        group = jnp.concatenate(
            [
                across[8 * p + 2 : 8 * p + 3] * 64.0 + across[8 * p + 3 : 8 * p + 4]
                for p in range(parts)
            ],
            axis=1,
        )
        picker = one_hot(iota((cap, LOW), 1, F32) == key_low)
        options = jnp.dot(picker, table_wide[...], preferred_element_type=F32)
        fetched = jnp.zeros((cap, width), F32)
        wide_high = jnp.broadcast_to(key_high, (cap, width))
        for h in range(high):
            fetched = jnp.where(
                wide_high == float(h), options[:, h * width : (h + 1) * width], fetched
            )
        joined = (payload * fetched).astype(BF16)
        picker = one_hot(iota((groups, cap), 0, F32) == group)
        terms = jnp.dot(picker, joined, preferred_element_type=F32)
        if started:
            acc[...] += terms
        else:
            acc[...] = terms

    join_block(send_buf, 0, False)

    @pl.loop(1, devices)
    def _(step):
        row_copy(step).wait_recv()
        join_block(recv_buf, step, True)

    acc_send[...] = acc[...].astype(BF16)

    def part_copy(step):
        to = partner(step)
        return pltpu.make_async_remote_copy(
            src_ref=acc_send.at[pl.ds(pl.multiple_of(to * GRP_DEV, GRP_DEV), GRP_DEV)],
            dst_ref=part_recv.at[step],
            send_sem=part_send_sem.at[step],
            recv_sem=part_recv_sem.at[step],
            device_id=address(to),
            device_id_type=MESH,
        )

    @pl.loop(1, devices)
    def _(step):
        part_copy(step).start()

    sums_ref[...] = acc[pl.ds(pl.multiple_of(me * GRP_DEV, GRP_DEV), GRP_DEV), :]

    @pl.loop(1, devices)
    def _(step):
        row_copy(step).wait_send()

    @pl.loop(1, devices)
    def _(step):
        part_copy(step).wait_recv()
        sums_ref[...] += part_recv[step].astype(F32)

    score = jnp.sum(sums_ref[...], axis=1, keepdims=True) / width
    spot = (GRP_DEV, BLOCK)
    across = jnp.sum(
        jnp.where(iota(spot, 0) == iota(spot, 1), score, 0.0), axis=0, keepdims=True
    )
    across = jnp.where(lane < GRP_DEV, across, -jnp.inf)
    score_send[...] = jnp.broadcast_to(across, score_send.shape)
    score_recv[0] = score_send[...]

    def score_copy(step):
        return pltpu.make_async_remote_copy(
            src_ref=score_send,
            dst_ref=score_recv.at[step],
            send_sem=score_send_sem.at[step],
            recv_sem=score_recv_sem.at[step],
            device_id=address(partner(step)),
            device_id_type=MESH,
        )

    @pl.loop(1, devices)
    def _(step):
        score_copy(step).start()

    @pl.loop(1, devices)
    def _(step):
        part_copy(step).wait_send()

    @pl.loop(1, devices)
    def _(step):
        score_copy(step).wait_recv()

    scores = score_recv[:, 0, :]
    spots = iota((1, BLOCK), 1, F32)
    top = jnp.zeros((1, BLOCK), F32)
    filled = jnp.zeros((1, 1), F32)
    limit = None
    for _ in range(TOPK):
        left = scores if limit is None else jnp.where(scores < limit, scores, -jnp.inf)
        limit = jnp.max(jnp.max(left, axis=0, keepdims=True), axis=1, keepdims=True)
        top = jnp.where(spots >= filled, limit, top)
        same = jnp.where(scores == limit, 1.0, 0.0)
        filled = filled + jnp.sum(
            jnp.sum(same, axis=0, keepdims=True), axis=1, keepdims=True
        )
    top_ref[...] = top

    @pl.loop(1, devices)
    def _(step):
        score_copy(step).wait_send()


def on_device(
    devices,
    inner,
    measures,
    pred_columns,
    bounds,
    lengths,
    destination,
    key_offset,
    group_ids,
    build_table,
):
    rows, width = measures.shape
    blocks = rows // BLOCK
    cap = max(BLOCK, 2 * rows // devices)
    parts = cap // BLOCK
    meta_rows = 16 * ((parts * 8 + 15) // 16)
    slot_rows = cap + meta_rows
    groups = GRP_DEV * devices
    vmem = pl.BlockSpec(memory_space=pltpu.VMEM)
    smem = pl.BlockSpec(memory_space=pltpu.SMEM)
    sums, top = pl.pallas_call(
        functools.partial(kernel, devices, inner, cap),
        out_shape=(
            jax.ShapeDtypeStruct((GRP_DEV, width), F32),
            jax.ShapeDtypeStruct((1, BLOCK), F32),
        ),
        in_specs=[smem, smem] + [vmem] * 6,
        out_specs=(vmem, vmem),
        scratch_shapes=[
            pltpu.VMEM((cap, rows), BF16),
            pltpu.VMEM((rows, width), BF16),
            pltpu.VMEM((devices * 8, rows), BF16),
            pltpu.VMEM((devices, meta_rows, BLOCK), BF16),
            pltpu.VMEM((LOW, build_table.shape[0] // LOW * width), BF16),
            pltpu.VMEM((devices, slot_rows, width), BF16),
            pltpu.VMEM((devices, slot_rows, width), BF16),
            pltpu.VMEM((groups, width), F32),
            pltpu.VMEM((groups, width), BF16),
            pltpu.VMEM((devices, GRP_DEV, width), BF16),
            pltpu.VMEM((8, BLOCK), F32),
            pltpu.VMEM((devices, 8, BLOCK), F32),
        ]
        + [pltpu.SemaphoreType.DMA((devices,))] * 6,
        compiler_params=pltpu.CompilerParams(
            collective_id=0, has_side_effects=True, vmem_limit_bytes=56 * 1024 * 1024
        ),
    )(
        bounds,
        lengths,
        measures,
        pred_columns,
        destination.reshape(blocks, BLOCK),
        key_offset.reshape(blocks, BLOCK),
        group_ids.reshape(blocks, BLOCK),
        build_table,
    )
    return (sums, top[0, :TOPK])


def solution(mesh):
    both = ("section", "dom")
    inner = mesh.shape["dom"]
    devices = mesh.shape["section"] * inner
    return jax.shard_map(
        functools.partial(on_device, devices, inner),
        mesh=mesh,
        in_specs=(
            P(both, None),
            P(None, both),
            P(),
            P(both),
            P(both, None),
            P(both),
            P(both),
            P(both, None),
        ),
        out_specs=(P(both, None), P()),
        check_vma=False,
    )
```

time: 352 us -> 82.4 us (0.23)
  waiting for transfers between devices: 182 us -> 0 us
  Pallas kernels: 0 us -> 79.1 us
  blocking collectives: 36.9 us -> 0 us
  matrix products: 32.8 us -> 0 us
  local copies, waits for them, and re-layouts: 35 us -> 2.49 us
  other arithmetic: 31.2 us -> 0 us
  starting transfers between devices: 19 us -> 0 us
  between operations: 14.2 us -> 0.65 us
    reduce_scatter x1 -> x0, waiting for transfers between devices: 132 us -> none  [on_device(): lax.psum_scatter(group_terms(joined, received_groups, GRP_DEV * lax.axis_...]
    pallas_call x0 -> x1, Pallas kernels: none -> 79.1 us  [on_device(): pl.pallas_call(functools.partial(kernel, devices, inner, cap), out_shape=...]
    all_to_all x3 -> x0, waiting for transfers between devices: 49.8 us -> none  [the longest x1 49.8 us: on_device(): lax.all_to_all(shaped[0], ('section', 'dom'), split_axis=0, concat_axis=0...]
    unnamed x1 -> x0, blocking collectives: 36.9 us -> none
    dot_general x16 -> x0, matrix products: 32.8 us -> none  [the longest x8 17.7 us: one_block(): fetched = jnp.dot(picker, build_table, preferred_element_type=jnp.float32)]
    scatter x2 -> x0, local copies, waits for them, and re-layouts: 32.5 us -> none  [the longest x1 16.3 us: fill_slots(): jnp.zeros((total_slots,), jnp.int32).at[places].set(second_ints)]
    all_to_all x3 -> x0, starting transfers between devices: 19 us -> none  [the longest x1 7.3 us: on_device(): lax.all_to_all(shaped[1], ('section', 'dom'), split_axis=0, concat_axis=0...]
    scatter x1 -> x0, other arithmetic: 14.6 us -> none  [fill_slots(): jnp.zeros((total_slots, payload.shape[1]), payload.dtype).at[places]]
  transfers between devices with their start and end apart: 4 -> 0, of which waited for: 2 -> 0; matrix products, arithmetic and copies ran while one was open for 9% -> 0% of each run, Pallas kernels for 0% -> 0%
where the time goes in v1:
time: 82.4 us; the launch traced here: 82.2 us
  Pallas kernels  79.1 us (96%)
  local copies, waits for them, and re-layouts  2.49 us (3%)
    pallas_call x1, Pallas kernels, on_device(): pl.pallas_call(functools.partial(kernel, devices, inner, cap), out_shape=...  79.1 us
    unnamed x3, local copies, waits for them, and re-layouts  1.98 us

profile of v1, /device:TPU:0, one launch (start us, length us, event | category | flops | bytes accessed | tf_op | source)
XLA Modules:
  0.0 82.2 jit_solution(6966765371129051687)
XLA Ops:
  0.6 79.1 %shard_map.95 = (f32[32,128]{1,0:T(8,128)}, f32[1,128]{1,0:T(1,128)}) custom-call(s32[2,2]{1,0:T(2,128)} %bounds_ref.1, s32[32]{0:T(128)} %lengths_ref.1, bf16[4096,128]{1,0:T(8,128)(2,1)} %x_ref.1, s32[2,4096]{1,0:T(2,128)} %pred_ref.1, s32[32,128]{1,0:T(8,128)} %bitcast.5, s32[32,128]{1,0:T(8,128)} %bitcast.6, s32[32,128]{1,0:T(8,128)} %bitcast.7, ...), custom_call_target="tpu_custom_call" | custom-call | tf_op jit(solution)/shard_map/pallas_call | solution.py:313
  79.7 0.0 copy-start
  79.7 0.7 copy-done
  80.4 0.5 slice_bitcast_fusion
  80.9 1.3 %copy.11 = f32[32,128]{1,0:T(8,128)} copy(f32[32,128]{1,0:T(8,128)} %get-tuple-element.8) | data formatting | bytes 32768
Async XLA Ops:
  79.7 0.7 copy-start

commit v2 on v1

--- a/solution.py
+++ b/solution.py
@@ -12,6 +12,7 @@
 GRP_DEV = 32
 STRIDE = 11
 LOW = 256
+CORES = 2
 MESH = pl.DeviceIdType.MESH
 F32 = jnp.float32
 BF16 = jnp.bfloat16
@@ -51,6 +52,9 @@
     part_recv,
     score_send,
     score_recv,
+    shards,
+    shard_send_sem,
+    shard_recv_sem,
     send_sem,
     recv_sem,
     part_send_sem,
@@ -78,6 +82,65 @@
         pl.semaphore_signal(
             barrier, inc=1, device_id=address(partner(step)), device_id_type=MESH
         )
+
+    sections = devices // inner
+    depth = inner // CORES
+    peers = sections * CORES
+    section = lax.axis_index("section")
+    level = lax.div(lax.axis_index("dom"), CORES)
+    core = lax.rem(lax.axis_index("dom"), CORES)
+
+    def shard_copy(source, shard, way):
+        return pltpu.make_async_remote_copy(
+            src_ref=source,
+            dst_ref=shards.at[shard],
+            send_sem=shard_send_sem.at[way, shard],
+            recv_sem=shard_recv_sem.at[shard],
+            device_id=(
+                section,
+                lax.rem(level + 1 + way * (depth - 2), depth) * CORES + core,
+            ),
+            device_id_type=MESH,
+        )
+
+    def shard_round(distance):
+        below = level - distance
+        above = level + distance
+
+        @pl.when(below >= 0)
+        def _():
+            shard_copy(shards.at[below], below, 0).wait_recv()
+
+            @pl.when(level + 1 < depth)
+            def _():
+                shard_copy(shards.at[below], below, 0).start()
+
+        @pl.when(above < depth)
+        def _():
+            shard_copy(shards.at[above], above, 1).wait_recv()
+
+            @pl.when(level > 0)
+            def _():
+                shard_copy(shards.at[above], above, 1).start()
+
+    def level_at(place):
+        far = lax.div(place + 1, 2)
+        near = jnp.where(lax.rem(place, 2) == 1, level - far, level + far)
+        upper = depth - 1 - level
+        rest = jnp.where(level < upper, place, depth - 1 - place)
+        return jnp.where(place <= 2 * jnp.minimum(level, upper), near, rest)
+
+    pl.semaphore_wait(barrier, devices - 1)
+
+    @pl.when(level + 1 < depth)
+    def _():
+        shard_copy(table_ref, level, 0).start()
+
+    @pl.when(level > 0)
+    def _():
+        shard_copy(table_ref, level, 1).start()
+
+    acc[...] = jnp.zeros_like(acc)
 
     names = iota((devices, BLOCK), 0)
     matches = [
@@ -133,43 +196,55 @@
         if parts * 8 < meta_rows:
             tiles.append(jnp.zeros((meta_rows - parts * 8, BLOCK), F32))
         meta_tiles[d] = jnp.concatenate(tiles, axis=0).astype(BF16)
-    for h in range(high):
-        table_wide[:, h * width : (h + 1) * width] = table_ref[h * LOW : (h + 1) * LOW, :]
-
-    pl.semaphore_wait(barrier, devices - 1)
-
-    def row_copy(step):
+    def target(offset):
+        to = lax.rem(section + lax.div(offset, CORES), sections)
+        return to, lax.rem(core + lax.rem(offset, CORES), CORES)
+
+    def row_copy(slot, offset):
+        to, to_core = target(offset)
         return pltpu.make_async_remote_copy(
-            src_ref=send_buf.at[step],
-            dst_ref=recv_buf.at[step],
-            send_sem=send_sem.at[step],
-            recv_sem=recv_sem.at[step],
-            device_id=address(partner(step)),
+            src_ref=send_buf.at[slot],
+            dst_ref=recv_buf.at[slot],
+            send_sem=send_sem.at[slot],
+            recv_sem=recv_sem.at[slot],
+            device_id=(to, level * CORES + to_core),
             device_id_type=MESH,
         )
 
-    @pl.loop(0, devices // 2)
-    def _(index):
-        first = 2 * index + 1
-        second = lax.rem(first + 1, devices)
-        wide = dest_wide[...]
-        sides = []
-        for step in (first, second):
-            name = partner(step).astype(F32).astype(BF16)
-            sides.append(jnp.where(wide == name, x_ref[...], jnp.zeros((), BF16)))
-        placed = jnp.dot(
-            onehot[...], jnp.concatenate(sides, axis=1), preferred_element_type=F32
-        ).astype(BF16)
-        for at, step in enumerate((first, second)):
-            send_buf[step, 0:cap, :] = placed[:, at * width : (at + 1) * width]
-            send_buf[step, cap:, :] = meta_tiles[partner(step)]
-        row_copy(first).start()
-
-        @pl.when(second > 0)
-        def _():
-            row_copy(second).start()
-
-    def join_block(buf, step, started):
+    def send_rows(place):
+        owner_level = level_at(place)
+
+        @pl.loop(0, peers // 2)
+        def _(index):
+            base = peers - 2 - 2 * index
+            owners = []
+            for offset in (base, base + 1):
+                to, to_core = target(offset)
+                owners.append(to * inner + owner_level * CORES + to_core)
+            wide = dest_wide[...]
+            sides = []
+            for owner in owners:
+                name = owner.astype(F32).astype(BF16)
+                sides.append(jnp.where(wide == name, x_ref[...], jnp.zeros((), BF16)))
+            placed = jnp.dot(
+                onehot[...], jnp.concatenate(sides, axis=1), preferred_element_type=F32
+            ).astype(BF16)
+            for at, owner in enumerate(owners):
+                slot = owner_level * peers + base + at
+                send_buf[slot, 0:cap, :] = placed[:, at * width : (at + 1) * width]
+                send_buf[slot, cap:, :] = meta_tiles[owner]
+            slot = owner_level * peers + base
+            row_copy(slot + 1, base + 1).start()
+
+            @pl.when(base > 0)
+            def _():
+                row_copy(slot, base).start()
+
+            @pl.when(base == 0)
+            def _():
+                recv_buf[slot] = send_buf[slot]
+
+    def join_block(buf, step):
         payload = buf[step, 0:cap, :].astype(F32)
         tile = buf[step, cap:, :]
         across = tile.astype(F32)
@@ -198,17 +273,56 @@
         joined = (payload * fetched).astype(BF16)
         picker = one_hot(iota((groups, cap), 0, F32) == group)
         terms = jnp.dot(picker, joined, preferred_element_type=F32)
-        if started:
-            acc[...] += terms
-        else:
-            acc[...] = terms
-
-    join_block(send_buf, 0, False)
-
-    @pl.loop(1, devices)
-    def _(step):
-        row_copy(step).wait_recv()
-        join_block(recv_buf, step, True)
+        acc[...] += terms
+
+    def widen(source):
+        for h in range(high):
+            table_wide[:, h * width : (h + 1) * width] = source[h * LOW : (h + 1) * LOW, :]
+
+    early = min(2, depth)
+
+    @pl.loop(0, early)
+    def _(place):
+        send_rows(place)
+
+    if depth > 1:
+        shard_round(1)
+
+    @pl.loop(early, depth)
+    def _(place):
+        send_rows(place)
+
+    @pl.loop(0, depth)
+    def _(place):
+        if depth > 2:
+
+            @pl.when((place >= 1) & (place + 1 < depth - 1))
+            def _():
+                shard_round(place + 1)
+
+            @pl.when(place == depth - 1)
+            def _():
+                shard_round(depth - 1)
+
+        owner_level = level_at(place)
+
+        @pl.when(place == 0)
+        def _():
+            widen(table_ref)
+
+        @pl.when(place > 0)
+        def _():
+            widen(shards.at[owner_level])
+
+        @pl.loop(0, peers)
+        def _(offset):
+            slot = owner_level * peers + offset
+
+            @pl.when(offset > 0)
+            def _():
+                row_copy(slot, offset).wait_recv()
+
+            join_block(recv_buf, slot)
 
     acc_send[...] = acc[...].astype(BF16)
 
@@ -229,9 +343,19 @@
 
     sums_ref[...] = acc[pl.ds(pl.multiple_of(me * GRP_DEV, GRP_DEV), GRP_DEV), :]
 
-    @pl.loop(1, devices)
-    def _(step):
-        row_copy(step).wait_send()
+    @pl.loop(0, depth)
+    def _(at):
+        @pl.loop(1, peers)
+        def _(offset):
+            row_copy(at * peers + offset, offset).wait_send()
+
+        @pl.when((at <= level) & (level + 1 < depth))
+        def _():
+            shard_copy(shards.at[at], at, 0).wait_send()
+
+        @pl.when((at >= level) & (level > 0))
+        def _():
+            shard_copy(shards.at[at], at, 1).wait_send()
 
     @pl.loop(1, devices)
     def _(step):
@@ -331,6 +455,9 @@
             pltpu.VMEM((devices, GRP_DEV, width), BF16),
             pltpu.VMEM((8, BLOCK), F32),
             pltpu.VMEM((devices, 8, BLOCK), F32),
+            pltpu.VMEM((inner // CORES,) + build_table.shape, BF16),
+            pltpu.SemaphoreType.DMA((2, inner // CORES)),
+            pltpu.SemaphoreType.DMA((inner // CORES,)),
         ]
         + [pltpu.SemaphoreType.DMA((devices,))] * 6,
         compiler_params=pltpu.CompilerParams(

time: 82.4 us -> 75.2 us (0.913)
  Pallas kernels: 79.1 us -> 71.8 us
    pallas_call x1, Pallas kernels: 79.1 us -> 71.8 us  [on_device(): pl.pallas_call(functools.partial(kernel, devices, inner, cap), out_shape=...]
where the time goes in v2:
time: 75.2 us; the launch traced here: 75 us
  Pallas kernels  71.8 us (95%)
  local copies, waits for them, and re-layouts  2.49 us (3%)
    pallas_call x1, Pallas kernels, on_device(): pl.pallas_call(functools.partial(kernel, devices, inner, cap), out_shape=...  71.8 us
    unnamed x3, local copies, waits for them, and re-layouts  1.98 us

profile of v2, /device:TPU:0, one launch (start us, length us, event | category | flops | bytes accessed | tf_op | source)
XLA Modules:
  0.0 75.0 jit_solution(8992100790017511866)
XLA Ops:
  0.6 71.8 %shard_map.95 = (f32[32,128]{1,0:T(8,128)}, f32[1,128]{1,0:T(1,128)}) custom-call(s32[2,2]{1,0:T(2,128)} %bounds_ref.1, s32[32]{0:T(128)} %lengths_ref.1, bf16[4096,128]{1,0:T(8,128)(2,1)} %x_ref.1, s32[2,4096]{1,0:T(2,128)} %pred_ref.1, s32[32,128]{1,0:T(8,128)} %bitcast.5, s32[32,128]{1,0:T(8,128)} %bitcast.6, s32[32,128]{1,0:T(8,128)} %bitcast.7, ...), custom_call_target="tpu_custom_call" | custom-call | tf_op jit(solution)/shard_map/pallas_call | solution.py:437
  72.4 0.0 copy-start
  72.5 0.7 copy-done
  73.1 0.5 slice_bitcast_fusion
  73.6 1.3 %copy.11 = f32[32,128]{1,0:T(8,128)} copy(f32[32,128]{1,0:T(8,128)} %get-tuple-element.8) | data formatting | bytes 32768
Async XLA Ops:
  72.4 0.7 copy-start

commit v3 on v2

--- a/solution.py
+++ b/solution.py
@@ -41,7 +41,8 @@
     sums_ref,
     top_ref,
     onehot,
-    dest_wide,
+    spread,
+    inner_wide,
     masked_meta,
     meta_tiles,
     table_wide,
@@ -155,6 +156,10 @@
     lane = iota((1, BLOCK), 1)
     diagonal = iota((BLOCK, BLOCK), 0) == iota((BLOCK, BLOCK), 1)
     ones = jnp.ones((BLOCK, BLOCK), BF16)
+    spread_slots = iota((sections * cap, BLOCK), 0, F32)
+    dest_section = lax.div(dest_ref[...], inner)
+    dest_inner = (dest_ref[...] - dest_section * inner).astype(F32)
+    section_base = dest_section.astype(F32) * cap
     for b in range(blocks):
         part = counts[b * devices : (b + 1) * devices]
         place = (
@@ -168,10 +173,11 @@
             usable = usable & (values >= bounds_ref[c, 0]) & (values < bounds_ref[c, 1])
         place = jnp.where(usable, place, -1.0)
         onehot[:, columns] = one_hot(slots == place)
-        dest_row = dest_ref[b : b + 1, :].astype(F32)
-        dest_diag = jnp.where(diagonal, dest_row, 0.0).astype(BF16)
-        dest_wide[columns, :] = jnp.dot(
-            dest_diag, ones, preferred_element_type=F32
+        place = jnp.where(usable, place + section_base[b : b + 1], -1.0)
+        spread[:, columns] = one_hot(spread_slots == place)
+        inner_diag = jnp.where(diagonal, dest_inner[b : b + 1], 0.0).astype(BF16)
+        inner_wide[columns, :] = jnp.dot(
+            inner_diag, ones, preferred_element_type=F32
         ).astype(BF16)
         key = key_ref[b : b + 1, :]
         group = group_ref[b : b + 1, :]
@@ -213,67 +219,69 @@
 
     def send_rows(place):
         owner_level = level_at(place)
-
-        @pl.loop(0, peers // 2)
+        sides = []
+        for c in range(CORES):
+            name = (owner_level * CORES + c).astype(F32).astype(BF16)
+            sides.append(
+                jnp.where(inner_wide[...] == name, x_ref[...], jnp.zeros((), BF16))
+            )
+        placed = jnp.dot(
+            spread[...], jnp.concatenate(sides, axis=1), preferred_element_type=F32
+        ).astype(BF16)
+        for to in range(sections):
+            for c in range(CORES):
+                offset = lax.rem(to - section + sections, sections) * CORES + lax.rem(
+                    c - core + CORES, CORES
+                )
+                slot = owner_level * peers + offset
+                send_buf[slot, 0:cap, :] = placed[
+                    to * cap : (to + 1) * cap, c * width : (c + 1) * width
+                ]
+                send_buf[slot, cap:, :] = meta_tiles[
+                    to * inner + owner_level * CORES + c
+                ]
+
+        @pl.loop(1, peers)
         def _(index):
-            base = peers - 2 - 2 * index
-            owners = []
-            for offset in (base, base + 1):
-                to, to_core = target(offset)
-                owners.append(to * inner + owner_level * CORES + to_core)
-            wide = dest_wide[...]
-            sides = []
-            for owner in owners:
-                name = owner.astype(F32).astype(BF16)
-                sides.append(jnp.where(wide == name, x_ref[...], jnp.zeros((), BF16)))
-            placed = jnp.dot(
-                onehot[...], jnp.concatenate(sides, axis=1), preferred_element_type=F32
-            ).astype(BF16)
-            for at, owner in enumerate(owners):
-                slot = owner_level * peers + base + at
-                send_buf[slot, 0:cap, :] = placed[:, at * width : (at + 1) * width]
-                send_buf[slot, cap:, :] = meta_tiles[owner]
-            slot = owner_level * peers + base
-            row_copy(slot + 1, base + 1).start()
-
-            @pl.when(base > 0)
-            def _():
-                row_copy(slot, base).start()
-
-            @pl.when(base == 0)
-            def _():
-                recv_buf[slot] = send_buf[slot]
-
-    def join_block(buf, step):
-        payload = buf[step, 0:cap, :].astype(F32)
-        tile = buf[step, cap:, :]
-        across = tile.astype(F32)
-        down = lax.dot_general(
-            one_hot(diagonal), tile, (((1,), (1,)), ((), ())), preferred_element_type=F32
-        )
-        key_high = jnp.concatenate([down[:, 8 * p : 8 * p + 1] for p in range(parts)], axis=0)
-        key_low = jnp.concatenate(
-            [down[:, 8 * p + 1 : 8 * p + 2] for p in range(parts)], axis=0
-        )
-        group = jnp.concatenate(
-            [
-                across[8 * p + 2 : 8 * p + 3] * 64.0 + across[8 * p + 3 : 8 * p + 4]
-                for p in range(parts)
-            ],
-            axis=1,
-        )
-        picker = one_hot(iota((cap, LOW), 1, F32) == key_low)
+            offset = peers - index
+            row_copy(owner_level * peers + offset, offset).start()
+
+        recv_buf[owner_level * peers] = send_buf[owner_level * peers]
+
+    def join_blocks(first, batch):
+        payload, key_high, key_low, group = [], [], [], []
+        for at in range(batch):
+            payload.append(recv_buf[first + at, 0:cap, :])
+            tile = recv_buf[first + at, cap:, :]
+            across = tile.astype(F32)
+            down = lax.dot_general(
+                one_hot(diagonal),
+                tile,
+                (((1,), (1,)), ((), ())),
+                preferred_element_type=F32,
+            )
+            for p in range(parts):
+                key_high.append(down[:, 8 * p : 8 * p + 1])
+                key_low.append(down[:, 8 * p + 1 : 8 * p + 2])
+                group.append(
+                    across[8 * p + 2 : 8 * p + 3] * 64.0 + across[8 * p + 3 : 8 * p + 4]
+                )
+        payload = jnp.concatenate(payload, axis=0).astype(F32)
+        key_high = jnp.concatenate(key_high, axis=0)
+        key_low = jnp.concatenate(key_low, axis=0)
+        group = jnp.concatenate(group, axis=1)
+        size = batch * cap
+        picker = one_hot(iota((size, LOW), 1, F32) == key_low)
         options = jnp.dot(picker, table_wide[...], preferred_element_type=F32)
-        fetched = jnp.zeros((cap, width), F32)
-        wide_high = jnp.broadcast_to(key_high, (cap, width))
+        fetched = jnp.zeros((size, width), F32)
+        wide_high = jnp.broadcast_to(key_high, (size, width))
         for h in range(high):
             fetched = jnp.where(
                 wide_high == float(h), options[:, h * width : (h + 1) * width], fetched
             )
         joined = (payload * fetched).astype(BF16)
-        picker = one_hot(iota((groups, cap), 0, F32) == group)
-        terms = jnp.dot(picker, joined, preferred_element_type=F32)
-        acc[...] += terms
+        picker = one_hot(iota((groups, size), 0, F32) == group)
+        acc[...] += jnp.dot(picker, joined, preferred_element_type=F32)
 
     def widen(source):
         for h in range(high):
@@ -314,15 +322,19 @@
         def _():
             widen(shards.at[owner_level])
 
-        @pl.loop(0, peers)
-        def _(offset):
-            slot = owner_level * peers + offset
-
-            @pl.when(offset > 0)
-            def _():
-                row_copy(slot, offset).wait_recv()
-
-            join_block(recv_buf, slot)
+        batch = min(4, peers)
+
+        @pl.loop(0, peers // batch)
+        def _(index):
+            base = index * batch
+            for at in range(batch):
+                offset = base + at
+
+                @pl.when(offset > 0)
+                def _():
+                    row_copy(owner_level * peers + offset, offset).wait_recv()
+
+            join_blocks(owner_level * peers + base, batch)
 
     acc_send[...] = acc[...].astype(BF16)
 
@@ -444,6 +456,7 @@
         out_specs=(vmem, vmem),
         scratch_shapes=[
             pltpu.VMEM((cap, rows), BF16),
+            pltpu.VMEM((devices // inner * cap, rows), BF16),
             pltpu.VMEM((rows, width), BF16),
             pltpu.VMEM((devices * 8, rows), BF16),
             pltpu.VMEM((devices, meta_rows, BLOCK), BF16),

time: 75.2 us -> 68.8 us (0.915)
  Pallas kernels: 71.8 us -> 65.4 us
    pallas_call x1, Pallas kernels: 71.8 us -> 65.4 us  [on_device(): pl.pallas_call(functools.partial(kernel, devices, inner, cap), out_shape=...]
where the time goes in v3:
time: 68.8 us; the launch traced here: 68.6 us
  Pallas kernels  65.4 us (95%)
  local copies, waits for them, and re-layouts  2.49 us (4%)
    pallas_call x1, Pallas kernels, on_device(): pl.pallas_call(functools.partial(kernel, devices, inner, cap), out_shape=...  65.4 us
    unnamed x3, local copies, waits for them, and re-layouts  1.98 us

profile of v3, /device:TPU:0, one launch (start us, length us, event | category | flops | bytes accessed | tf_op | source)
XLA Modules:
  0.0 68.6 jit_solution(7035971486713727129)
XLA Ops:
  0.6 65.4 %shard_map.95 = (f32[32,128]{1,0:T(8,128)}, f32[1,128]{1,0:T(1,128)}) custom-call(s32[2,2]{1,0:T(2,128)} %bounds_ref.1, s32[32]{0:T(128)} %lengths_ref.1, bf16[4096,128]{1,0:T(8,128)(2,1)} %x_ref.1, s32[2,4096]{1,0:T(2,128)} %pred_ref.1, s32[32,128]{1,0:T(8,128)} %bitcast.5, s32[32,128]{1,0:T(8,128)} %bitcast.6, s32[32,128]{1,0:T(8,128)} %bitcast.7, ...), custom_call_target="tpu_custom_call" | custom-call | tf_op jit(solution)/shard_map/pallas_call | solution.py:449
  66.1 0.0 copy-start
  66.1 0.7 copy-done
  66.7 0.5 slice_bitcast_fusion
  67.3 1.3 %copy.11 = f32[32,128]{1,0:T(8,128)} copy(f32[32,128]{1,0:T(8,128)} %get-tuple-element.8) | data formatting | bytes 32768
Async XLA Ops:
  66.1 0.7 copy-start
